TPU v7x, 512 devices: a whole 4x4x16 slice. The times are simulated.
512 devices in a mesh: mp: 4 (over z_hi), space: 128 (over x, z_lo, y, core).
Axes of the slice: x: 4, y: 4, z: 16 (z_hi: 4, z_lo: 4; z = z_hi * 4 + z_lo), core: 2. Of those that a mesh axis runs over, the one named last changes fastest.
Arguments:
- density: float32 [4, 8192, 128], P('mp', 'space'), may hold values from 0.5 to 2
- fields: float32 [4, 7, 8192, 128], P('mp', None, 'space'), may hold values from -3 to 3
- src_points: int32 [4, 128, 128, 64], P('mp', 'space'), may hold values from 0 to 8191
- dst_points: int32 [4, 128, 128, 64], P('mp', 'space'), may hold values from 0 to 8191, as said below
- recv_count: int32 [4, 128, 128], P('mp', 'space'), may hold values from 16 to 64, as said below
- iono_owner: int32 [16384], replicated, may hold values from 0 to 255, as said below
- iono_cell: int32 [16384], replicated, may hold values from 0 to 8191
- response: bfloat16 [16384, 16384], P(('mp', 'space')), may hold values from -0.046875 to 0.046875
Outputs:
- density_out: float32 [4, 8192, 128], P('mp', 'space')
- fields_out: float32 [4, 7, 8192, 128], P('mp', None, 'space')
Inputs may be any that keep to these rules, and one draw needn't show every extreme that they name: Within one block of the receiving section the cells dst_points[s, k, :, :] are all different. `recv_count`: in every section one block receives all 64 slots from every block of the section before it. `iono_owner`: magnetosphere blocks are numbered (section - 2) * 128 + block; no two ionosphere points share both owner and cell.
All inputs are finite; a program needn't handle non-finite values.
Results may differ from a plain program's by a relative error of at most 0.0003.
Values sent between devices are 32-bit elements; how exact they have to be, the bound alone decides.
A program may use at most 64 MiB of HBM per device.

v0:
```python
import jax
import jax.numpy as jnp
from jax import lax
from jax.sharding import PartitionSpec as P

TIME_STEPS = 2


LAMBDA_STEP = 0.1
SOUND_SPEED = 1.0


def from_behind(value, axis, steps):
    count = lax.axis_size(axis)
    initial, last = (max(0, -steps), min(count, count - steps))
    return lax.ppermute(value, axis, [(source, source + steps) for source in range(initial, last)])


def with_halo(value, sides, width):
    for axis, dim in sides:
        devices, length = (lax.axis_size(axis), value.shape[dim])
        up = [(i, (i + 1) % devices) for i in range(devices)]
        down = [(j, i) for i, j in up]
        last = lax.slice_in_dim(value, length - width, length, axis=dim)
        initial = lax.slice_in_dim(value, 0, width, axis=dim)
        before = lax.ppermute(last, axis, up)
        after = lax.ppermute(initial, axis, down)
        value = jnp.concatenate([before, value, after], axis=dim)
    return value


def slice_span(array_in, start_at, trim_end, axis_dim):
    return lax.slice_in_dim(array_in, start_at, array_in.shape[axis_dim] - trim_end, axis=axis_dim)


def advance(padded, speed_row, axis_dim):
    velocity = padded[speed_row] / padded[0]
    flux_all = padded * velocity[None]
    lower_speed = jnp.abs(slice_span(velocity, 0, 1, axis_dim - 1))
    upper_speed = jnp.abs(slice_span(velocity, 1, 0, axis_dim - 1))
    signal_speed = jnp.maximum(lower_speed, upper_speed) + SOUND_SPEED
    face_flux = 0.5 * (
        slice_span(flux_all, 0, 1, axis_dim) + slice_span(flux_all, 1, 0, axis_dim)
    ) - 0.5 * signal_speed[None] * (
        slice_span(padded, 1, 0, axis_dim) - slice_span(padded, 0, 1, axis_dim)
    )
    return slice_span(padded, 1, 1, axis_dim) - LAMBDA_STEP * (
        slice_span(face_flux, 1, 0, axis_dim) - slice_span(face_flux, 0, 1, axis_dim)
    )


def column_sweep(block_state):
    padded = jnp.concatenate([block_state[:, :, :1], block_state, block_state[:, :, -1:]], axis=2)
    return advance(padded, 1, 2)


def local(density, fields, src_points, dst_points, recv_count, iono_owner, iono_cell, response):
    plasma_state = jnp.concatenate([density, fields[0]], axis=0)
    components, block_rows, block_cols = plasma_state.shape
    block_cells = block_rows * block_cols
    points = src_points.shape[-1]
    section = lax.axis_index("mp")
    place_index = lax.axis_index("space")
    space_count = lax.axis_size("space")
    flat_start = plasma_state.reshape(components, block_cells)
    outgoing = flat_start[:, src_points[0, 0].reshape(-1)]
    spread = lax.all_to_all(outgoing, "space", split_axis=1, concat_axis=1, tiled=True)
    arrived = from_behind(spread, "mp", 1)
    magnetic = plasma_state[6]
    column_edges = jnp.concatenate([magnetic[:, :1], magnetic, magnetic[:, -1:]], axis=1)
    current_local = (0.5 * (column_edges[:, 2:] - column_edges[:, :-2])).reshape(-1)
    owner_self = jnp.where(section >= 2, (section - 2) * space_count + place_index, -1)
    owned_points = iono_owner == owner_self
    contribution = jnp.where(owned_points, current_local[iono_cell], 0.0)
    current_total = lax.psum(contribution, ("mp", "space"))
    potential_rows = jnp.dot(
        response.astype(jnp.float32),
        current_total,
        precision=lax.Precision.HIGHEST,
        preferred_element_type=jnp.float32,
    )
    potential = lax.all_gather(potential_rows, ("mp", "space"), axis=0, tiled=True)
    advanced = plasma_state
    for substep in range(TIME_STEPS):
        advanced = column_sweep(advanced)
        widened = with_halo(advanced, (("space", 1),), 1)
        advanced = advance(widened, 2, 1)
    slot_index = jnp.arange(points)
    usable = (slot_index[None, :] < recv_count[0, 0][:, None]) & (section > 0)
    target = jnp.where(usable, dst_points[0, 0], block_cells).reshape(-1)
    flat_end = advanced.reshape(components, block_cells).at[:, target].set(arrived, mode="drop")
    spot = jnp.where(owned_points, iono_cell, block_cells)
    drift_push = 0.5 * flat_end[0][iono_cell] * potential
    flat_end = flat_end.at[1, spot].add(drift_push, mode="drop")
    result = flat_end.reshape(components, block_rows, block_cols)
    return (result[:1], result[1:][None])


def solution(mesh):
    placed = (
        P("mp", "space", None),
        P("mp", None, "space", None),
        P("mp", "space", None, None),
        P("mp", "space", None, None),
        P("mp", "space", None),
        P(),
        P(),
        P(("mp", "space"), None),
    )
    return jax.shard_map(
        local,
        mesh=mesh,
        in_specs=placed,
        out_specs=(P("mp", "space", None), P("mp", None, "space", None)),
        check_vma=False,
    )
```

profile of v0, /device:TPU:481, one launch (start us, length us, event | category | flops | bytes accessed | tf_op | source)
XLA Modules:
  0.0 1144.1 jit_solution(17041225057414486299)
XLA Ops:
  7.2 1.3 fusion.12
  11.0 1.4 fusion.3
  12.6 3.8 collective-permute-start
  16.4 1.9 collective-permute-start.1
  18.5 2.6 copy.28
  21.4 29.9 %gather_fusion = f32[8192,8]{1,0:T(8,128)} fusion(f32[8,8192]{0,1:T(8,128)} %copy.28, s32[8192]{0:T(1024)S(1)} %broadcast_clamp_fusion), kind=kCustom, calls=%fused_computation | custom fusion | bytes 557056 | tf_op jit(solution)/shard_map/gather | solution.py:66
  51.3 2.8 copy.29
  55.2 13.4 %all-to-all-start = ((f32[128,1,512]{2,1,0:T(1,128)}), f32[128,1,512]{2,1,0:T(1,128)S(1)}, u32[]{:S(2)}, u32[]{:S(2)}) async-start(f32[128,1,512]{2,1,0:T(1,128)} %reshape.182), calls=%async_computation | async-start | bytes 524288 | tf_op jit(solution)/shard_map/all_to_all | solution.py:67
  68.9 90.5 %gather_fusion.2 = f32[16384]{0:T(1024)S(1)} fusion(f32[8192]{0:T(1024)S(1)} %fusion.43, s32[16384]{0:T(1024)S(1)} %fusion.23), kind=kCustom, calls=%fused_computation.2 | custom fusion | bytes 196608 | tf_op jit(solution)/shard_map/gather | solution.py:74
  163.0 3.4 collective-permute-start.2
  166.4 1.9 collective-permute-start.3
  168.3 3.0 collective-permute-done.3
  172.1 1.3 reduce.6
  173.8 1.5 collective-permute-start.4
  175.3 2.6 copy.25
  177.9 430.8 %all-reduce.5.cloned.1.call-done = f32[16384]{0:T(1024)} async-done(((f32[16384]{0:T(1024)}), f32[16384]{0:T(1024)}) %all-reduce.5.cloned.1.call-update) | async-done | bytes 65552 | tf_op jit(solution)/shard_map/psum | solution.py:75
  608.7 1.7 convolution_bitcast_fusion
  611.4 2.6 copy.31
  614.0 24.9 %scatter_fusion = f32[8,8192]{0,1:T(8,128)} fusion(f32[8,8192]{0,1:T(8,128)} %bitcast.49, s32[8192]{0:T(1024)S(1)} %bitcast.65, f32[8192,8]{1,0:T(8,128)} %copy.31), kind=kCustom, calls=%fused_computation.3 | custom fusion | bytes 819200 | tf_op jit(solution)/shard_map/scatter | solution.py:91
  639.0 3.3 slice_reduce_fusion
  642.3 2.8 copy.32
  645.1 90.5 %gather_fusion.1 = f32[16384]{0:T(1024)S(1)} fusion(f32[8192]{0:T(1024)S(1)} %slice_reduce_fusion, s32[16384]{0:T(1024)S(1)} %fusion.23), kind=kCustom, calls=%fused_computation.1 | custom fusion | bytes 196608 | tf_op jit(solution)/shard_map/gather | solution.py:93
  735.7 311.5 %all-reduce.7.cloned.1.call-done = f32[16384]{0:T(1024)} async-done(((f32[16384]{0:T(1024)}), f32[16384]{0:T(1024)}) %all-reduce.7.cloned.1.call-update) | async-done | bytes 65552
  1048.0 87.9 %scatter_fusion.1 = f32[65536]{0:T(1024)S(1)} fusion(f32[65536]{0:T(1024)S(1)} %bitcast.48, s32[16384]{0:T(1024)S(1)} %broadcast_select_fusion.1, f32[16384]{0:T(1024)S(1)} %multiply_multiply_fusion), kind=kCustom, calls=%fused_computation.4 | custom fusion | flops 16384 | bytes 262144
  (90 shorter events, 12.1 us)
Async XLA Ops:
  7.2 601.5 %copy-start = (bf16[32,16384]{1,0:T(8,128)(2,1)S(1)}, bf16[32,16384]{1,0:T(8,128)(2,1)}, u32[]{:S(2)}) copy-start(bf16[32,16384]{1,0:T(8,128)(2,1)} %param.15) | copy-start | bytes 3145732
  7.2 5.3 copy-start.1
  7.2 5.3 copy-start.2
  11.0 10.1 copy-start.6
  12.6 148.7 %collective-permute-start = (f32[8,1,128]{2,1,0:T(1,128)S(1)}, f32[8,1,128]{2,1,0:T(1,128)S(1)}, u32[]{:S(2)}, u32[]{:S(2)}) collective-permute-start(f32[8,1,128]{2,1,0:T(1,128)S(1)} %get-tuple-element.8), channel_id=1, source_target_pairs={{0,1},{1,2},{2,3},{3,4},{4,5},{5,6},{6,7},{7,8},{8,9},{9,10},{10,1... | collective-permute-start | bytes 12296 | tf_op jit(solution)/shard_map/ppermute | solution.py:26
  16.4 145.0 %collective-permute-start.1 = (f32[8,1,128]{2,1,0:T(1,128)S(1)}, f32[8,1,128]{2,1,0:T(1,128)S(1)}, u32[]{:S(2)}, u32[]{:S(2)}) collective-permute-start(f32[8,1,128]{2,1,0:T(1,128)S(1)} %get-tuple-element.9), channel_id=1, source_target_pairs={{1,0},{2,1},{3,2},{4,3},{5,4},{6,5},{7,6},{8,7},{9,8},{10,9},{11,1... | collective-permute-start | bytes 12296 | tf_op jit(solution)/shard_map/ppermute | solution.py:27
  21.4 47.3 %copy-start.3 = (s32[16384]{0:T(1024)S(1)}, s32[16384]{0:T(1024)}, u32[]{:S(2)}) copy-start(s32[16384]{0:T(1024)} %param.14) | copy-start | bytes 196612
  55.2 116.4 %all-to-all-start = ((f32[128,1,512]{2,1,0:T(1,128)}), f32[128,1,512]{2,1,0:T(1,128)S(1)}, u32[]{:S(2)}, u32[]{:S(2)}) async-start(f32[128,1,512]{2,1,0:T(1,128)} %reshape.182), calls=%async_computation | async-start | bytes 524288 | tf_op jit(solution)/shard_map/all_to_all | solution.py:67
  68.6 540.1 %all-reduce.5.cloned.1.call-start = ((), (), s32[]{:S(2)}) async-start(), calls=%async_computation.1 | async-start | bytes 131072 | tf_op jit(solution)/shard_map/psum | solution.py:75
  68.9 90.6 %copy-start.5 = (s32[16384]{0:T(1024)S(1)}, s32[16384]{0:T(1024)}, u32[]{:S(2)}) copy-start(s32[16384]{0:T(1024)} %param.13) | copy-start | bytes 196612
  68.9 91.3 %copy-start.10 = (s32[1,1,128]{2,1,0:T(1,128)S(1)}, s32[1,1,128]{2,1,0:T(1,128)}, u32[]{:S(2)}) copy-start(s32[1,1,128]{2,1,0:T(1,128)} %param.12) | copy-start | bytes 1540
  68.9 91.5 %copy-start.7 = (s32[1,1,128,64]{2,3,1,0:T(8,128)S(1)}, s32[1,1,128,64]{2,3,1,0:T(8,128)}, u32[]{:S(2)}) copy-start(s32[1,1,128,64]{2,3,1,0:T(8,128)} %param.11) | copy-start | bytes 98308
  68.9 91.8 %copy-start.9 = (s32[2]{0:T(128)S(1)}, s32[2]{0:T(128)}, u32[]{:S(2)}) copy-start(s32[2]{0:T(128)} %constant.52) | copy-start | bytes 28
  68.9 92.1 %copy-start.8 = (s32[2]{0:T(128)S(1)}, s32[2]{0:T(128)}, u32[]{:S(2)}) copy-start(s32[2]{0:T(128)} %constant.49) | copy-start | bytes 28
  160.2 887.0 %all-reduce.7.cloned.1.call-start = ((), (), s32[]{:S(2)}) async-start(), calls=%async_computation.2 | async-start | bytes 131072
  163.0 5.3 collective-permute-start.2
  166.4 4.9 collective-permute-start.3
  173.8 437.6 %collective-permute-start.4 = (f32[8,8192]{1,0:T(8,128)S(1)}, f32[8,8192]{1,0:T(8,128)S(1)}, u32[]{:S(2)}, u32[]{:S(2)}) collective-permute-start(f32[8,8192]{1,0:T(8,128)S(1)} %all_to_all.10), channel_id=1, source_target_pairs={{0,128},{128,256},{256,384},{1,129},{129,257},{257,385},{2,130},{1... | collective-permute-start | bytes 786440 | tf_op jit(solution)/shard_map/ppermute | solution.py:16
  610.7 0.6 copy-start.4
Sparse Core Ops, SparseCore 0:
  160.3 448.3 all-reduce.4
  615.6 431.5 all-reduce.6
where the time goes:
time: 1150 us; the launch traced here: 1140 us
  waiting for transfers between devices  745 us (65%)
  local copies, waits for them, and re-layouts  258 us (22%)
  other arithmetic  98.7 us (9%)
  starting transfers between devices  25.9 us (2%)
  between operations  14.7 us (1%)
    psum x1, waiting for transfers between devices, local(): current_total = lax.psum(contribution, ('mp', 'space'))  431 us
    unnamed x3, waiting for transfers between devices  312 us
    gather x1, local copies, waits for them, and re-layouts, local(): drift_push = 0.5 * flat_end[0][iono_cell] * potential  90.5 us
    gather x1, local copies, waits for them, and re-layouts, local(): contribution = jnp.where(owned_points, current_local[iono_cell], 0.0)  90.5 us
    unnamed x4, other arithmetic  88.5 us
    gather x1, local copies, waits for them, and re-layouts, local(): outgoing = flat_start[:, src_points[0, 0].reshape(-1)]  29.9 us
    scatter x2, local copies, waits for them, and re-layouts, local(): advanced.reshape(components, block_cells).at[:, target]  27.7 us
  transfers between devices with their start and end apart: 8, of which 3 were waited for; matrix products, arithmetic and copies ran while one was open for 23% of the time, Pallas kernels for 0%

commit v1 on v0

v1 whole, which is shorter than its diff:
```python
import functools

import jax
import jax.numpy as jnp
from jax import lax
from jax.experimental import pallas as pl
from jax.experimental.pallas import tpu as pltpu
from jax.sharding import PartitionSpec as P

MESH = pl.DeviceIdType.MESH
YC = 8
XZ = 16
LAMBDA_STEP = 0.1
F32 = jnp.float32
I32 = jnp.int32
BF16 = jnp.bfloat16


def iota(shape, dim):
    return lax.broadcasted_iota(I32, shape, dim)


def pick(tables, count, row, lane):
    shape = row.shape

    def step(r, held):
        hit = row == r
        return tuple(
            jnp.where(
                hit,
                jnp.take_along_axis(jnp.broadcast_to(line, shape), lane, axis=1, mode="promise_in_bounds"),
                old,
            )
            for line, old in zip(tables(r), held)
        )

    start = tuple(jnp.zeros(shape, F32) for _ in tables(0))
    return lax.fori_loop(0, count, step, start, unroll=4)


def pack_kernel(density, fields, src, owner, cell, outbox, contribution, state, index, current):
    mp = lax.axis_index("mp")
    me = (mp - 2) * (XZ * YC) + lax.axis_index("space")
    low = iota((8, 128), 1) < 64
    state[0] = density[0]
    for c in range(7):
        state[c + 1] = fields[0, c]

    @pl.when(mp >= 2)
    def _():
        b = state[6]
        col = iota((64, 128), 1)
        right = jnp.where(col == 127, b, pltpu.roll(b, 127, 1))
        left = jnp.where(col == 0, b, pltpu.roll(b, 1, 1))
        current[...] = 0.5 * (right - left)
        for half in range(2):
            part = pl.ds(half * 64, 64)
            cells = cell[part, :]
            (got,) = pick(lambda r: (current[pl.ds(r, 1), :],), 64, cells >> 7, cells & 127)
            contribution[part, :] = jnp.where(owner[part, :] == me, got, 0.0)

    @pl.when(mp < 3)
    def _():
        points = src[...]
        turned = jnp.concatenate([points, points], axis=0).T
        index[...] = jnp.where(iota((64, 128), 1) < 64, turned[:64], turned[64:])

        def block(b, carry):
            cells = index[pl.ds(b * 16, 16), :]
            got = pick(lambda r: tuple(state[c, pl.ds(r, 1), :] for c in range(8)), 64, cells >> 7, cells & 127)
            for half in range(2):
                for q in range(4):
                    first = got[2 * q][half * 8 : half * 8 + 8]
                    second = got[2 * q + 1][half * 8 : half * 8 + 8]
                    xz = b * 2 + half
                    outbox[pl.ds(xz * 4 + q, 8, stride=64), :] = jnp.where(low, first, pltpu.roll(second, 64, 1))
                    outbox[pl.ds((xz + 8) * 4 + q, 8, stride=64), :] = jnp.where(low, pltpu.roll(first, 64, 1), second)
            return carry

        lax.fori_loop(0, 4, block, 0)


def invert(rows_ref, used, high_of, low_of, count):
    def step(b, total):
        cells = rows_ref[pl.ds(b * 8, 8), :]
        keep = used(b)
        row8 = jnp.where(keep, cells >> 7, -1)
        col8 = cells & 127
        left, right = [], []
        for s in range(8):
            hit = iota((64, 128), 0) == row8[s : s + 1]
            left.append(
                jnp.concatenate(
                    [jnp.where(hit, high_of(b * 8 + s), 0.0), jnp.where(hit, low_of(b * 8 + s), 0.0)], axis=0
                ).astype(BF16)
            )
            right.append(jnp.where(iota((128, 128), 0) == col8[s : s + 1], 1.0, 0.0).astype(BF16))
        return total + lax.dot_general(
            jnp.concatenate(left, axis=1),
            jnp.concatenate(right, axis=1),
            (((1,), (1,)), ((), ())),
            preferred_element_type=F32,
        )

    return lax.fori_loop(0, count // 8, step, jnp.zeros((128, 128), F32))


def sweep(work, speed, axis):
    shape = (80, 128)
    size = shape[axis]
    at = iota(shape, axis)

    def above(value):
        moved = pltpu.roll(value, size - 1, axis)
        return jnp.where(at == size - 1, value, moved) if axis == 1 else moved

    u = work[speed] / work[0]
    u_up = above(u)
    fast = 0.5 * (jnp.maximum(jnp.abs(u), jnp.abs(u_up)) + 1.0)
    for c in range(8):
        q = work[c]
        flux = u * q
        face = 0.5 * (flux + above(flux)) - fast * (above(q) - q)
        below = pltpu.roll(face, 1, axis)
        if axis == 1:
            below = jnp.where(at == 0, flux, below)
        work[c] = q - LAMBDA_STEP * (face - below)


def wait_for(ref, sem):
    pltpu.make_async_copy(ref, ref, sem).wait()


def exchange_kernel(
    density, fields, dst, recv_count, owner, cell, response, outbox, contribution,
    swept, inbox_out, potential, slot_code, iono_code,
    work, halo_out, halo_in, mid, inbox, rs, part, ar, full, spread, line, lines, tile, pot_part, pot,
    halo_send, halo_recv, send, rs_recv, ar_recv, full_recv, mid_recv, inbox_recv, line_recv, pot_recv,
):
    mp = lax.axis_index("mp")
    space = lax.axis_index("space")
    xz = lax.div(space, YC)
    yc = lax.rem(space, YC)
    magnetic = mp >= 2
    a_me = mp * YC + yc
    size = XZ * YC

    def a_device(a):
        return (lax.div(a, YC), xz * YC + lax.rem(a, YC))

    def b_device(x):
        return (mp, x * YC + yc)

    def loop(first, last, body):
        def step(i, carry):
            body(i)
            return carry

        lax.fori_loop(first, last, step, 0)

    barrier = pltpu.get_barrier_semaphore()

    def greet(device):
        pl.semaphore_signal(barrier, inc=1, device_id=device, device_id_type=MESH)

    after = (mp, lax.rem(space + 1, size))
    before = (mp, lax.rem(space + size - 1, size))
    greet(after)
    greet(before)
    loop(1, XZ, lambda i: greet(b_device(lax.rem(xz + i, XZ))))
    loop(1, 4 * YC, lambda i: greet(a_device(lax.rem(a_me + i, 4 * YC))))

    work[...] = jnp.ones_like(work)
    work[0, 8:72, :] = density[0]
    for c in range(7):
        work[c + 1, 8:72, :] = fields[0, c]
    for c in range(8):
        for i in range(2):
            halo_out[0, pl.ds(i * 8 + c, 1), :] = work[c, 8 + i : 9 + i, :]
            halo_out[1, pl.ds(i * 8 + c, 1), :] = work[c, 70 + i : 71 + i, :]

    pl.semaphore_wait(barrier, 2 + XZ - 1 + 4 * YC - 1)

    def push(src_ref, dst_ref, send_sem, recv_sem, device):
        pltpu.make_async_remote_copy(
            src_ref=src_ref, dst_ref=dst_ref, send_sem=send_sem, recv_sem=recv_sem,
            device_id=device, device_id_type=MESH,
        ).start()

    @pl.when(magnetic)
    def _():
        def one(i):
            to = lax.rem(xz + i, XZ)
            push(contribution.at[to], rs.at[xz], send.at[0], rs_recv, b_device(to))

        loop(1, XZ, one)
        rs[xz] = contribution[xz]

    push(halo_out.at[0], halo_in.at[1], halo_send.at[0], halo_recv.at[1], before)
    push(halo_out.at[1], halo_in.at[0], halo_send.at[1], halo_recv.at[0], after)

    @pl.when(mp < 3)
    def _():
        def one(i):
            to = lax.rem(yc + i, YC)
            push(outbox.at[to], mid.at[yc], send.at[1], mid_recv, (mp + 1, xz * YC + to))

        loop(0, YC, one)

    @pl.when(magnetic)
    def _():
        wait_for(rs.at[pl.ds(0, XZ - 1)], rs_recv)
        total = rs[0]
        for i in range(1, XZ):
            total = total + rs[i]
        part[...] = total
        mine = a_me - 2 * YC

        def one(i):
            push(part, ar.at[mine], send.at[2], ar_recv, a_device(lax.rem(a_me + i, 4 * YC)))

        loop(1, 4 * YC, one)
        ar[mine] = total

    lane = iota((1, 128), 1)

    @pl.when(mp > 0)
    def _():
        counts = recv_count[...]
        high = ((lane & 63) + 1).astype(F32)

        def used(b):
            return (iota((8, 128), 0) + b * 8) < counts

        def low(p):
            return ((lane >> 6) * 64 + p).astype(F32)

        slot_code[...] = invert(dst, used, lambda p: high, low, 64).astype(I32)

    wait_for(halo_in.at[0], halo_recv.at[0])
    wait_for(halo_in.at[1], halo_recv.at[1])
    for c in range(8):
        for i in range(2):
            work[c, 6 + i : 7 + i, :] = halo_in[0, pl.ds(i * 8 + c, 1), :]
            work[c, 72 + i : 73 + i, :] = halo_in[1, pl.ds(i * 8 + c, 1), :]

    @pl.when(magnetic)
    def _():
        wait_for(ar.at[pl.ds(0, 2 * YC - 1)], ar_recv)

    @pl.when(mp < 2)
    def _():
        wait_for(ar.at[pl.ds(0, 2 * YC)], ar_recv)

    total = ar[0]
    for i in range(1, 2 * YC):
        total = total + ar[i]
    full[...] = total

    def give(i):
        push(full, spread.at[xz], send.at[3], full_recv, b_device(lax.rem(xz + i, XZ)))

    loop(1, XZ, give)
    spread[xz] = total

    for _ in range(2):
        sweep(work, 1, 1)
        sweep(work, 2, 0)
    swept[...] = work[:, 8:72, :]

    wait_for(spread.at[pl.ds(0, XZ - 1)], full_recv)
    acc = jnp.zeros((32, 128), F32)
    for i in range(128):
        acc = acc + response[:, i * 128 : (i + 1) * 128].astype(F32) * spread[i // 8, i % 8 : i % 8 + 1, :]
    tile[...] = jnp.zeros_like(tile)
    tile[pl.ds(pl.multiple_of(lax.rem(yc, 4) * 32, 32), 32), :] = acc
    line[...] = jnp.sum(tile[...].T, axis=0, keepdims=True)

    @pl.when(magnetic)
    def _():
        mine = a_me - 2 * YC

        def one(i):
            to = lax.rem(mine + i, 2 * YC)
            push(line, lines.at[a_me], send.at[4], line_recv, a_device(to + 2 * YC))

        loop(1, 2 * YC, one)
        lines[a_me] = line[...]

    @pl.when(mp < 2)
    def _():
        def one(i):
            to = lax.rem(yc + i, 2 * YC)
            push(line, lines.at[a_me], send.at[4], line_recv, a_device(to + 2 * YC))

        loop(0, 2 * YC, one)

    @pl.when(mp > 0)
    def _():
        wait_for(mid, mid_recv)

        def one(i):
            to = lax.rem(xz + i, XZ)
            push(mid.at[:, to], inbox.at[xz], send.at[5], inbox_recv, b_device(to))

        loop(1, XZ, one)
        inbox[xz] = mid[:, xz]

    @pl.when(magnetic)
    def _():
        me = (mp - 2) * size + space

        def used(b):
            return owner[pl.ds(b * 8, 8), :] == me

        def high(i):
            return ((lax.rem(lax.div(i, 2), 16) * 8 + lax.div(i, 32) * 2 + lax.rem(i, 2)) + 1).astype(F32)

        low = lane.astype(F32)
        iono_code[...] = invert(cell, used, high, lambda i: low, 128).astype(I32)

        wait_for(lines.at[pl.ds(0, 4 * YC - 1)], line_recv)
        rows = []
        for m in range(4):
            for h in range(2):
                row = lines[m * 8 + h * 4]
                for i in range(1, 4):
                    row = row + lines[m * 8 + h * 4 + i]
                rows.append(row)
        mine = jnp.concatenate(rows, axis=0)
        pot_part[...] = mine

        def one(i):
            push(pot_part, pot.at[xz], send.at[6], pot_recv, b_device(lax.rem(xz + i, XZ)))

        loop(1, XZ, one)
        pot[xz] = mine
        wait_for(pot.at[pl.ds(0, XZ - 1)], pot_recv)
        potential[...] = pot[...]

    @pl.when(mp > 0)
    def _():
        wait_for(inbox.at[pl.ds(0, XZ - 1)], inbox_recv)
        inbox_out[...] = inbox[...]

    wait_for(halo_out.at[0], halo_send.at[0])
    wait_for(halo_out.at[1], halo_send.at[1])
    wait_for(spread.at[pl.ds(0, XZ - 1)], send.at[3])

    @pl.when(mp < 3)
    def _():
        wait_for(mid, send.at[1])

    @pl.when(mp > 0)
    def _():
        wait_for(inbox.at[pl.ds(0, XZ - 1)], send.at[5])

    @pl.when(magnetic)
    def _():
        wait_for(rs.at[pl.ds(0, XZ - 1)], send.at[0])
        wait_for(ar.at[pl.ds(0, 4 * YC - 1)], send.at[2])
        wait_for(lines.at[pl.ds(0, 2 * YC - 1)], send.at[4])
        wait_for(pot.at[pl.ds(0, XZ - 1)], send.at[6])

    @pl.when(mp < 2)
    def _():
        wait_for(lines.at[pl.ds(0, 2 * YC)], send.at[4])


def place_kernel(swept, inbox, potential, slot_code, iono_code, density_out, fields_out, state, table):
    mp = lax.axis_index("mp")
    low = iota((8, 128), 1) < 64

    @pl.when(mp == 0)
    def _():
        state[...] = swept[...]

    @pl.when(mp > 0)
    def _():
        for b in range(8):
            for q in range(4):
                first = inbox[pl.ds(b * 32 + q, 8, stride=4), :]
                second = inbox[pl.ds((b + 8) * 32 + q, 8, stride=4), :]
                table[2 * q, b * 8 : b * 8 + 8, :] = jnp.where(low, first, pltpu.roll(second, 64, 1))
                table[2 * q + 1, b * 8 : b * 8 + 8, :] = jnp.where(low, pltpu.roll(first, 64, 1), second)

        def block(b, carry):
            part = pl.ds(b * 16, 16)
            row = slot_code[part, :] - 1
            lane = slot_code[pl.ds(64 + b * 16, 16), :]
            got = pick(lambda r: tuple(table[c, pl.ds(r, 1), :] for c in range(8)), 64, row, lane)
            for c in range(8):
                state[c, part, :] = jnp.where(row >= 0, got[c], swept[c, part, :])
            return carry

        lax.fori_loop(0, 4, block, 0)

    @pl.when(mp >= 2)
    def _():
        row = iono_code[:64, :] - 1
        lane = iono_code[64:, :]
        (got,) = pick(lambda r: (potential[pl.ds(r, 1), :],), 128, row, lane)
        state[1] = state[1] + jnp.where(row >= 0, 0.5 * state[0] * got, 0.0)

    density_out[0] = state[0]
    for c in range(7):
        fields_out[0, c] = state[c + 1]


VMEM = pl.BlockSpec(memory_space=pltpu.VMEM)


def local(density, fields, src_points, dst_points, recv_count, iono_owner, iono_cell, response):
    src = src_points[0, 0].T
    dst = dst_points[0, 0].T
    owner = iono_owner.reshape(128, 128)
    cell = iono_cell.reshape(128, 128)
    outbox, contribution = pl.pallas_call(
        pack_kernel,
        out_shape=[jax.ShapeDtypeStruct((512, 128), F32), jax.ShapeDtypeStruct((128, 128), F32)],
        in_specs=[VMEM] * 5,
        out_specs=[VMEM] * 2,
        scratch_shapes=[
            pltpu.VMEM((8, 64, 128), F32),
            pltpu.VMEM((64, 128), I32),
            pltpu.VMEM((64, 128), F32),
        ],
        compiler_params=pltpu.CompilerParams(vmem_limit_bytes=24 * 1024 * 1024),
        name="pack",
    )(density, fields, src, owner, cell)
    dma = pltpu.SemaphoreType.DMA
    swept, inbox, potential, slot_code, iono_code = pl.pallas_call(
        exchange_kernel,
        out_shape=[
            jax.ShapeDtypeStruct((8, 64, 128), F32),
            jax.ShapeDtypeStruct((XZ, YC, 4, 128), F32),
            jax.ShapeDtypeStruct((XZ, 8, 128), F32),
            jax.ShapeDtypeStruct((128, 128), I32),
            jax.ShapeDtypeStruct((128, 128), I32),
        ],
        in_specs=[VMEM] * 9,
        out_specs=[VMEM] * 5,
        scratch_shapes=[
            pltpu.VMEM((8, 80, 128), F32),
            pltpu.VMEM((2, 16, 128), F32),
            pltpu.VMEM((2, 16, 128), F32),
            pltpu.VMEM((YC, XZ, 4, 128), F32),
            pltpu.VMEM((XZ, YC, 4, 128), F32),
            pltpu.VMEM((XZ, 8, 128), F32),
            pltpu.VMEM((8, 128), F32),
            pltpu.VMEM((4 * YC, 8, 128), F32),
            pltpu.VMEM((8, 128), F32),
            pltpu.VMEM((XZ, 8, 128), F32),
            pltpu.VMEM((1, 128), F32),
            pltpu.VMEM((4 * YC, 1, 128), F32),
            pltpu.VMEM((128, 128), F32),
            pltpu.VMEM((8, 128), F32),
            pltpu.VMEM((XZ, 8, 128), F32),
            dma((2,)),
            dma((2,)),
            dma((7,)),
            dma,
            dma,
            dma,
            dma,
            dma,
            dma,
            dma,
        ],
        compiler_params=pltpu.CompilerParams(
            collective_id=0, has_side_effects=True, vmem_limit_bytes=24 * 1024 * 1024
        ),
        name="exchange",
    )(
        density, fields, dst, recv_count[0], owner, cell, response,
        outbox.reshape(YC, XZ, 4, 128), contribution.reshape(XZ, 8, 128),
    )
    return pl.pallas_call(
        place_kernel,
        out_shape=[jax.ShapeDtypeStruct((1, 64, 128), F32), jax.ShapeDtypeStruct((1, 7, 64, 128), F32)],
        in_specs=[VMEM] * 5,
        out_specs=[VMEM] * 2,
        scratch_shapes=[pltpu.VMEM((8, 64, 128), F32), pltpu.VMEM((8, 64, 128), F32)],
        compiler_params=pltpu.CompilerParams(vmem_limit_bytes=24 * 1024 * 1024),
        name="place",
    )(swept, inbox.reshape(512, 128), potential.reshape(128, 128), slot_code, iono_code)


def solution(mesh):
    placed = (
        P("mp", "space", None),
        P("mp", None, "space", None),
        P("mp", "space", None, None),
        P("mp", "space", None, None),
        P("mp", "space", None),
        P(),
        P(),
        P(("mp", "space"), None),
    )
    return jax.shard_map(
        local,
        mesh=mesh,
        in_specs=placed,
        out_specs=(P("mp", "space", None), P("mp", None, "space", None)),
        check_vma=False,
    )
```

time: 1150 us -> 95.8 us (0.08)
  the two profiles are of different devices: /device:TPU:481 before, /device:TPU:352 now
where the time goes in v1:
time: 95.8 us; the launch traced here: 95.4 us
  Pallas kernels  88.7 us (93%)
  local copies, waits for them, and re-layouts  5.98 us (6%)
    pallas_call x1, Pallas kernels, local(): pl.pallas_call(exchange_kernel, out_shape=[jax.ShapeDtypeStruct((8, 64, 1...  59 us
    pallas_call x1, Pallas kernels, local(): pl.pallas_call(place_kernel, out_shape=[jax.ShapeDtypeStruct((1, 64, 128)...  15 us
    pallas_call x1, Pallas kernels, local(): pl.pallas_call(pack_kernel, out_shape=[jax.ShapeDtypeStruct((512, 128), F...  14.7 us
    unnamed x20, local copies, waits for them, and re-layouts  5.98 us

profile of v1, /device:TPU:352, one launch (start us, length us, event | category | flops | bytes accessed | tf_op | source)
XLA Modules:
  0.0 95.4 jit_solution(7465253250268639162)
XLA Ops:
  0.6 0.0 copy-start.1
  0.6 0.9 copy-done.1
  1.6 0.0 copy-start.2
  1.6 0.8 copy-done.2
  2.4 0.0 copy-start.4
  2.4 0.8 copy-done.4
  3.3 0.0 copy-start.6
  3.3 0.8 copy-done.6
  4.0 0.0 copy-start.8
  4.0 0.8 copy-done.8
  4.8 0.0 copy-start.3
  4.8 0.0 copy-start.5
  4.8 0.0 copy-start.7
  4.8 14.7 %pack.1 = (f32[512,128]{1,0:T(8,128)S(1)}, f32[128,128]{1,0:T(8,128)S(1)}) custom-call(f32[1,64,128]{2,1,0:T(8,128)S(1)} %copy-done.6, f32[1,7,64,128]{3,2,1,0:T(8,128)S(1)} %copy-done.1, s32[64,128]{1,0:T(8,128)S(1)} %bitcast.22, s32[128,128]{1,0:T(8,128)S(1)} %bitcast.13, s32[128,128]{1,0:T(8,128)S(1)} %bitcast.15), custom_call_target="tpu_custom_call" | custom-call | tf_op jit(solution)/shard_map/pack/pallas_call | solution.py:418
  19.5 0.0 copy-start.9
  19.5 0.0 copy-done.3
  19.5 0.0 copy-done.5
  19.5 0.0 copy-done.7
  19.6 0.6 copy-done.9
  20.2 0.0 copy-start
  20.2 1.2 %copy-done = bf16[32,16384]{1,0:T(8,128)(2,1)S(1)} copy-done((bf16[32,16384]{1,0:T(8,128)(2,1)S(1)}, bf16[32,16384]{1,0:T(8,128)(2,1)}, u32[]{:S(2)}) %copy-start) | copy-done | bytes 1048600
  21.4 59.0 %exchange.1 = (f32[8,64,128]{2,1,0:T(8,128)S(1)}, f32[16,8,4,128]{3,2,1,0:T(4,128)S(1)}, f32[16,8,128]{2,1,0:T(8,128)S(1)}, s32[128,128]{1,0:T(8,128)S(1)}, s32[128,128]{1,0:T(8,128)S(1)}) custom-call(f32[1,64,128]{2,1,0:T(8,128)S(1)} %copy-done.6, f32[1,7,64,128]{3,2,1,0:T(8,128)S(1)} %copy-done.1, s32[64,128]{1,0:T(8,128)S(1)} %bitcast.21, ...), custom_call_target="tpu_custom_call" | custom-call | tf_op jit(solution)/shard_map/exchange/pallas_call | solution.py:432
  80.4 15.0 %place.1 = (f32[1,64,128]{2,1,0:T(8,128)}, f32[1,7,64,128]{3,2,1,0:T(8,128)}) custom-call(f32[8,64,128]{2,1,0:T(8,128)S(1)} %get-tuple-element.11.swept, f32[512,128]{1,0:T(8,128)S(1)} %bitcast.17, f32[128,128]{1,0:T(8,128)S(1)} %bitcast.20, s32[128,128]{1,0:T(8,128)S(1)} %get-tuple-element.14.slot_code, s32[128,128]{1,0:T(8,128)S(1)} %get-tuple-element.15.iono_code), custom_call_target="tpu_custom_call" | custom-call | tf_op jit(solution)/shard_map/place/pallas_call | solution.py:478
Async XLA Ops:
  0.6 0.9 copy-start.1
  1.6 0.8 copy-start.2
  2.4 0.8 copy-start.4
  3.3 0.8 copy-start.6
  4.0 0.8 copy-start.8
  4.8 14.8 %copy-start.3 = (s32[16384]{0:T(1024)S(1)}, s32[16384]{0:T(1024)}, u32[]{:S(2)}) copy-start(s32[16384]{0:T(1024)} %param.13) | copy-start | bytes 196612
  4.8 14.8 %copy-start.5 = (s32[16384]{0:T(1024)S(1)}, s32[16384]{0:T(1024)}, u32[]{:S(2)}) copy-start(s32[16384]{0:T(1024)} %param.14) | copy-start | bytes 196612
  4.8 14.8 %copy-start.7 = (s32[1,1,128,64]{2,3,1,0:T(8,128)S(1)}, s32[1,1,128,64]{2,3,1,0:T(8,128)}, u32[]{:S(2)}) copy-start(s32[1,1,128,64]{2,3,1,0:T(8,128)} %param.11) | copy-start | bytes 98308
  19.5 0.7 copy-start.9
  20.2 1.2 %copy-start = (bf16[32,16384]{1,0:T(8,128)(2,1)S(1)}, bf16[32,16384]{1,0:T(8,128)(2,1)}, u32[]{:S(2)}) copy-start(bf16[32,16384]{1,0:T(8,128)(2,1)} %response.1) | copy-start | bytes 3145732

commit v2 on v0

v2 whole, which is shorter than its diff:
```python
import jax
import jax.numpy as jnp
from jax import lax
from jax.experimental import pallas as pl
from jax.experimental.pallas import tpu as pltpu
from jax.sharding import PartitionSpec as P

MESH = pl.DeviceIdType.MESH
YC = 8
ZS = 4
SPACE = 128
PLANE = 32
LEVELS = 16
LAMBDA_STEP = 0.1
F32 = jnp.float32
I32 = jnp.int32
BF16 = jnp.bfloat16


def iota(shape, dim):
    return lax.broadcasted_iota(I32, shape, dim)


def loop(first, last, body):
    def step(i, carry):
        body(i)
        return carry

    lax.fori_loop(first, last, step, 0)


def wait_for(ref, sem):
    pltpu.make_async_copy(ref, ref, sem).wait()


def push(src_ref, dst_ref, send_sem, recv_sem, device):
    pltpu.make_async_remote_copy(
        src_ref=src_ref,
        dst_ref=dst_ref,
        send_sem=send_sem,
        recv_sem=recv_sem,
        device_id=device,
        device_id_type=MESH,
    ).start()


def pick(lines, count, row, lane, held):
    shape = row.shape
    for r in range(count):
        hit = row == r
        held = [
            jnp.where(
                hit,
                jnp.take_along_axis(jnp.broadcast_to(line, shape), lane, axis=1, mode="promise_in_bounds"),
                old,
            )
            for line, old in zip(lines(r), held)
        ]
    return held


def invert(rows_ref, used, high_of, low_of, count):
    def step(b, total):
        cells = rows_ref[pl.ds(b * 8, 8), :]
        row8 = jnp.where(used(b), cells >> 7, -1)
        col8 = cells & 127
        left, right = [], []
        for s in range(8):
            hit = iota((64, 128), 0) == row8[s : s + 1]
            left.append(
                jnp.concatenate(
                    [jnp.where(hit, high_of(b * 8 + s), 0.0), jnp.where(hit, low_of(b * 8 + s), 0.0)], axis=0
                ).astype(BF16)
            )
            right.append(jnp.where(iota((128, 128), 0) == col8[s : s + 1], 1.0, 0.0).astype(BF16))
        return total + lax.dot_general(
            jnp.concatenate(left, axis=1),
            jnp.concatenate(right, axis=1),
            (((1,), (1,)), ((), ())),
            preferred_element_type=F32,
        )

    return lax.fori_loop(0, count // 8, step, jnp.zeros((128, 128), F32))


def sweep(work, speed, axis):
    shape = (80, 128)
    size = shape[axis]
    at = iota(shape, axis)

    def above(value):
        moved = pltpu.roll(value, size - 1, axis)
        return jnp.where(at == size - 1, value, moved) if axis == 1 else moved

    u = work[speed] / work[0]
    u_up = above(u)
    fast = 0.5 * (jnp.maximum(jnp.abs(u), jnp.abs(u_up)) + 1.0)
    for c in range(8):
        q = work[c]
        flux = u * q
        face = 0.5 * (flux + above(flux)) - fast * (above(q) - q)
        below = pltpu.roll(face, 1, axis)
        if axis == 1:
            below = jnp.where(at == 0, flux, below)
        work[c] = q - LAMBDA_STEP * (face - below)


def cycle_kernel(
    density_in, fields_in, src_in, dst_in, count_in, owner_in, cell_in, response_in,
    density_out, fields_out,
    work, src, dst, recv_count, owner, cell, response, index, current, halo_out, halo_in,
    outbox, mid, inbox, table, contribution, rs, part, ar, full, spread, tile, line, lines, pot_part, pot,
    slot_code, iono_code,
    load, halo_send, halo_recv, send, recv, out_send, mid_recv, fwd_send, inbox_recv,
):
    mp = lax.axis_index("mp")
    space = lax.axis_index("space")
    x = lax.div(space, ZS * YC)
    z = lax.rem(lax.div(space, YC), ZS)
    yc = lax.rem(space, YC)
    place = x * YC + yc
    level = mp * ZS + z
    magnetic = mp >= 2
    me = (mp - 2) * SPACE + space

    def in_plane(p):
        return (mp, (lax.div(p, YC) * ZS + z) * YC + lax.rem(p, YC))

    def in_column(l):
        return (lax.div(l, ZS), (x * ZS + lax.rem(l, ZS)) * YC + yc)

    body = pl.ds(8, 64)
    loads = [
        pltpu.make_async_copy(a, b, load.at[i])
        for i, (a, b) in enumerate(
            (
                (fields_in.at[0], work.at[pl.ds(1, 7), body]),
                (density_in.at[0], work.at[0, body]),
                (cell_in, cell),
                (owner_in, owner),
                (src_in, src),
                (dst_in, dst),
                (count_in, recv_count),
                (response_in, response),
            )
        )
    ]
    for copy in loads:
        copy.start()

    barrier = pltpu.get_barrier_semaphore()

    def greet(device):
        pl.semaphore_signal(barrier, inc=1, device_id=device, device_id_type=MESH)

    after = (mp, lax.rem(space + 1, SPACE))
    before = (mp, lax.rem(space + SPACE - 1, SPACE))
    loop(1, LEVELS, lambda i: greet(in_column(lax.rem(level + i, LEVELS))))
    loop(1, PLANE, lambda i: greet(in_plane(lax.rem(place + i, PLANE))))
    greet(after)
    greet(before)

    low = iota((8, 128), 1) < 64
    lane = iota((1, 128), 1)
    for copy in loads[:4]:
        copy.wait()
    for c in range(8):
        work[c, 0:8, :] = jnp.ones((8, 128), F32)
        work[c, 72:80, :] = jnp.ones((8, 128), F32)

    @pl.when(magnetic)
    def _():
        b = work[6, 8:72, :]
        col = iota((64, 128), 1)
        right = jnp.where(col == 127, b, pltpu.roll(b, 127, 1))
        left = jnp.where(col == 0, b, pltpu.roll(b, 1, 1))
        current[...] = 0.5 * (right - left)

        def block(b):
            at = pl.ds(b * 16, 16)
            cells = cell[at, :]
            (got,) = pick(lambda r: (current[r : r + 1, :],), 64, cells >> 7, cells & 127, [jnp.zeros((16, 128), F32)])
            got = jnp.where(owner[at, :] == me, got, 0.0)
            for i in range(4):
                contribution[b * 4 + i] = got[i * 4 : i * 4 + 4]

        loop(0, 8, block)

    for c in range(8):
        for i in range(2):
            halo_out[0, i * 8 + c : i * 8 + c + 1, :] = work[c, 8 + i : 9 + i, :]
            halo_out[1, i * 8 + c : i * 8 + c + 1, :] = work[c, 70 + i : 71 + i, :]
    loads[4].wait()

    @pl.when(mp < 3)
    def _():
        points = src[...]
        turned = jnp.concatenate([points, points], axis=0).T
        index[...] = jnp.where(iota((64, 128), 1) < 64, turned[:64], turned[64:])

    def pack(half):
        def block(b):
            cells = index[pl.ds(half * 32 + b * 16, 16), :]
            got = pick(
                lambda r: tuple(work[c, 8 + r : 9 + r, :] for c in range(8)),
                64, cells >> 7, cells & 127, [jnp.zeros((16, 128), F32)] * 8,
            )
            for i in range(2):
                for q in range(4):
                    first = got[2 * q][i * 8 : i * 8 + 8]
                    second = got[2 * q + 1][i * 8 : i * 8 + 8]
                    outbox[half, b * 2 + i, :, q, :] = jnp.where(low, first, pltpu.roll(second, 64, 1))
                    outbox[half + 2, b * 2 + i, :, q, :] = jnp.where(low, pltpu.roll(first, 64, 1), second)

        loop(0, 2, block)

    def depart(to_x, t):
        def one(i):
            to = lax.rem(z + i, ZS)
            push(outbox.at[to_x, to], mid.at[to_x, z], out_send, mid_recv.at[t], in_column((mp + 1) * ZS + to))

        loop(0, ZS, one)

    halves = (lax.rem(x + 1, 2), lax.rem(x, 2))

    @pl.when(mp < 3)
    def _():
        pack(halves[0])

    pl.semaphore_wait(barrier, LEVELS - 1 + PLANE - 1 + 2)

    @pl.when(magnetic)
    def _():
        def one(i):
            to = lax.rem(place + i, PLANE)
            push(contribution.at[to], rs.at[place], send.at[0], recv.at[0], in_plane(to))

        loop(PLANE // 2, PLANE, one)
        loop(1, PLANE // 2, one)
        rs[place] = contribution[place]

    push(halo_out.at[0], halo_in.at[1], halo_send.at[0], halo_recv.at[1], before)
    push(halo_out.at[1], halo_in.at[0], halo_send.at[1], halo_recv.at[0], after)

    @pl.when(mp < 3)
    def _():
        depart(halves[0], 0)
        depart(halves[0] + 2, 0)
        pack(halves[1])
        depart(lax.rem(x + 2, 4), 1)
        depart(x, 1)

    @pl.when(magnetic)
    def _():
        wait_for(rs.at[pl.ds(0, PLANE - 1)], recv.at[0])
        total = rs[0]
        for i in range(1, PLANE):
            total = total + rs[i]
        part[...] = total

        def one(i):
            push(part, ar.at[level - 8], send.at[1], recv.at[1], in_column(lax.rem(level + i, LEVELS)))

        loop(8, LEVELS, one)
        loop(1, 8, one)
        ar[level - 8] = total

    loads[5].wait()
    loads[6].wait()

    @pl.when(mp > 0)
    def _():
        counts = recv_count[...]
        high = ((lane & 63) + 1).astype(F32)

        def used(b):
            return (iota((8, 128), 0) + b * 8) < counts

        slot_code[...] = invert(dst, used, lambda p: high, lambda p: ((lane >> 6) * 64 + p).astype(F32), 64).astype(I32)

    for i in range(2):
        wait_for(halo_in.at[i], halo_recv.at[i])
    for c in range(8):
        for i in range(2):
            work[c, 6 + i : 7 + i, :] = halo_in[0, i * 8 + c : i * 8 + c + 1, :]
            work[c, 72 + i : 73 + i, :] = halo_in[1, i * 8 + c : i * 8 + c + 1, :]
    for _ in range(2):
        sweep(work, 1, 1)
        sweep(work, 2, 0)

    @pl.when(magnetic)
    def _():
        wait_for(ar.at[pl.ds(0, 7)], recv.at[1])

    @pl.when(mp < 2)
    def _():
        wait_for(ar.at[pl.ds(0, 8)], recv.at[1])

    total = ar[0]
    for i in range(1, 8):
        total = total + ar[i]
    full[...] = total

    def give(i):
        push(full, spread.at[place], send.at[2], recv.at[2], in_plane(lax.rem(place + i, PLANE)))

    loop(PLANE // 2, PLANE, give)
    loop(1, PLANE // 2, give)
    spread[place] = total

    @pl.when(magnetic)
    def _():
        def used(b):
            return owner[pl.ds(b * 8, 8), :] == me

        def high(i):
            row = lax.rem(lax.div(i, 8), 4) * 32 + lax.rem(i, 2) * 16 + lax.div(i, 32) + 1
            return (row + (lane >> 5) * 4).astype(F32)

        def low(i):
            return (lax.rem(lax.div(i, 2), 4) * 32 + (lane & 31)).astype(F32)

        iono_code[...] = invert(cell, used, high, low, 128).astype(I32)

    loads[7].wait()
    wait_for(spread.at[pl.ds(0, PLANE - 1)], recv.at[2])
    acc = jnp.zeros((32, 128), F32)
    for i in range(128):
        acc = acc + response[:, i * 128 : (i + 1) * 128].astype(F32) * spread[i // 4, i % 4 : i % 4 + 1, :]
    tile[...] = jnp.zeros_like(tile)
    tile[pl.ds(pl.multiple_of(z * 32, 32), 32), :] = acc
    line[...] = jnp.sum(tile[...].T, axis=0, keepdims=True)

    def report(i):
        push(line, lines.at[level], send.at[3], recv.at[3], in_column(8 + lax.rem(level + i, 8)))

    @pl.when(magnetic)
    def _():
        loop(1, 8, report)
        lines[level] = line[...]

    @pl.when(mp < 2)
    def _():
        loop(0, 8, report)

    def forward(to_x, t, first):
        def one(i):
            to = lax.rem(yc + i, YC)
            push(mid.at[to_x, :, to], inbox.at[x, :, yc], fwd_send.at[t], inbox_recv.at[t], in_plane(to_x * YC + to))

        loop(first, YC, one)

    @pl.when(mp > 0)
    def _():
        wait_for(mid.at[pl.ds(0, 2)], mid_recv.at[0])
        forward(halves[0], 0, 0)
        forward(halves[0] + 2, 0, 0)

    @pl.when(magnetic)
    def _():
        wait_for(lines.at[pl.ds(0, LEVELS - 1)], recv.at[3])
        rows = []
        for m in range(4):
            row = lines[m * 4]
            for i in range(1, 4):
                row = row + lines[m * 4 + i]
            rows.append(row)
        mine = jnp.concatenate(rows, axis=0)
        pot_part[...] = mine

        def one(i):
            push(pot_part, pot.at[place], send.at[4], recv.at[4], in_plane(lax.rem(place + i, PLANE)))

        loop(PLANE // 2, PLANE, one)
        loop(1, PLANE // 2, one)
        pot[place] = mine

    def unpack(half):
        for i in range(4):
            for q in range(4):
                first = inbox[half, i, :, q, :]
                second = inbox[half + 2, i, :, q, :]
                table[2 * q, i * 8 : i * 8 + 8, :] = jnp.where(low, first, pltpu.roll(second, 64, 1))
                table[2 * q + 1, i * 8 : i * 8 + 8, :] = jnp.where(low, pltpu.roll(first, 64, 1), second)

        def block(b):
            at = pl.ds(pl.multiple_of(8 + b * 16, 8), 16)
            row = slot_code[pl.ds(b * 16, 16), :] - (1 + half * 32)
            spot = slot_code[pl.ds(64 + b * 16, 16), :]
            got = pick(
                lambda r: tuple(table[c, r : r + 1, :] for c in range(8)),
                32, row, spot, [work[c, at, :] for c in range(8)],
            )
            for c in range(8):
                work[c, at, :] = got[c]

        loop(0, 4, block)

    @pl.when(mp > 0)
    def _():
        wait_for(mid.at[pl.ds(0, 2)], mid_recv.at[1])
        forward(lax.rem(x + 2, 4), 1, 0)
        forward(x, 1, 1)
        inbox[x, :, yc] = mid[x, :, yc]
        wait_for(inbox.at[pl.ds(0, 2)], inbox_recv.at[0])
        unpack(halves[0])
        wait_for(inbox.at[pl.ds(0, 3), :, pl.ds(0, 5)], inbox_recv.at[1])
        unpack(halves[1])

    @pl.when(magnetic)
    def _():
        wait_for(pot.at[pl.ds(0, PLANE - 1)], recv.at[4])

        def block(b):
            at = pl.ds(pl.multiple_of(8 + b * 16, 8), 16)
            row = iono_code[pl.ds(b * 16, 16), :] - 1
            spot = iono_code[pl.ds(64 + b * 16, 16), :]
            (got,) = pick(
                lambda r: (pot[r // 4, r % 4 : r % 4 + 1, :],), 128, row, spot, [jnp.zeros((16, 128), F32)]
            )
            work[1, at, :] = work[1, at, :] + jnp.where(row >= 0, 0.5 * work[0, at, :] * got, 0.0)

        loop(0, 4, block)

    results = [
        pltpu.make_async_copy(work.at[0, body], density_out.at[0], load.at[0]),
        pltpu.make_async_copy(work.at[pl.ds(1, 7), body], fields_out.at[0], load.at[1]),
    ]
    for copy in results:
        copy.start()

    for i in range(2):
        wait_for(halo_out.at[i], halo_send.at[i])
    wait_for(spread.at[pl.ds(0, PLANE - 1)], send.at[2])

    @pl.when(mp < 3)
    def _():
        wait_for(mid, out_send)

    @pl.when(mp > 0)
    def _():
        wait_for(inbox.at[pl.ds(0, 2)], fwd_send.at[0])
        wait_for(inbox.at[pl.ds(0, 3), :, pl.ds(0, 5)], fwd_send.at[1])

    @pl.when(magnetic)
    def _():
        wait_for(rs.at[pl.ds(0, PLANE - 1)], send.at[0])
        wait_for(ar.at[pl.ds(0, LEVELS - 1)], send.at[1])
        wait_for(lines.at[pl.ds(0, 7)], send.at[3])
        wait_for(pot.at[pl.ds(0, PLANE - 1)], send.at[4])

    @pl.when(mp < 2)
    def _():
        wait_for(lines.at[pl.ds(0, 8)], send.at[3])

    for copy in results:
        copy.wait()


def local(density, fields, src_points, dst_points, recv_count, iono_owner, iono_cell, response):
    vmem = pltpu.VMEM
    dma = pltpu.SemaphoreType.DMA
    hbm = pl.BlockSpec(memory_space=pl.ANY)
    return pl.pallas_call(
        cycle_kernel,
        out_shape=[jax.ShapeDtypeStruct((1, 64, 128), F32), jax.ShapeDtypeStruct((1, 7, 64, 128), F32)],
        in_specs=[hbm] * 8,
        out_specs=[hbm] * 2,
        scratch_shapes=[
            vmem((8, 80, 128), F32),
            vmem((64, 128), I32),
            vmem((64, 128), I32),
            vmem((1, 128), I32),
            vmem((128, 128), I32),
            vmem((128, 128), I32),
            vmem((32, 16384), BF16),
            vmem((64, 128), I32),
            vmem((64, 128), F32),
            vmem((2, 16, 128), F32),
            vmem((2, 16, 128), F32),
            vmem((4, ZS, YC, 4, 128), F32),
            vmem((4, ZS, YC, 4, 128), F32),
            vmem((4, ZS, YC, 4, 128), F32),
            vmem((8, 32, 128), F32),
            vmem((PLANE, 4, 128), F32),
            vmem((PLANE, 4, 128), F32),
            vmem((4, 128), F32),
            vmem((LEVELS, 4, 128), F32),
            vmem((4, 128), F32),
            vmem((PLANE, 4, 128), F32),
            vmem((128, 128), F32),
            vmem((1, 128), F32),
            vmem((LEVELS, 1, 128), F32),
            vmem((4, 128), F32),
            vmem((PLANE, 4, 128), F32),
            vmem((128, 128), I32),
            vmem((128, 128), I32),
            dma((8,)),
            dma((2,)),
            dma((2,)),
            dma((5,)),
            dma((5,)),
            dma,
            dma((2,)),
            dma((2,)),
            dma((2,)),
        ],
        compiler_params=pltpu.CompilerParams(
            collective_id=0, has_side_effects=True, vmem_limit_bytes=56 * 1024 * 1024
        ),
        name="cycle",
    )(
        density, fields, src_points[0, 0].T, dst_points[0, 0].T, recv_count[0],
        iono_owner.reshape(128, 128), iono_cell.reshape(128, 128), response,
    )


def solution(mesh):
    placed = (
        P("mp", "space", None),
        P("mp", None, "space", None),
        P("mp", "space", None, None),
        P("mp", "space", None, None),
        P("mp", "space", None),
        P(),
        P(),
        P(("mp", "space"), None),
    )
    return jax.shard_map(
        local,
        mesh=mesh,
        in_specs=placed,
        out_specs=(P("mp", "space", None), P("mp", None, "space", None)),
        check_vma=False,
    )
```

time: 1150 us -> 63.8 us (0.06)
  the two profiles are of different devices: /device:TPU:481 before, /device:TPU:257 now
where the time goes in v2:
time: 63.8 us; the launch traced here: 63.6 us
  Pallas kernels  59.9 us (94%)
  local copies, waits for them, and re-layouts  3.02 us (5%)
  between operations  0.64 us (1%)
    pallas_call x1, Pallas kernels, local(): pl.pallas_call(cycle_kernel, out_shape=[jax.ShapeDtypeStruct((1, 64, 128)...  59.9 us
    unnamed x2, local copies, waits for them, and re-layouts  3.02 us

profile of v2, /device:TPU:257, one launch (start us, length us, event | category | flops | bytes accessed | tf_op | source)
XLA Modules:
  0.0 63.6 jit_solution(4419086221840642085)
XLA Ops:
  0.6 59.9 %cycle.1 = (f32[1,64,128]{2,1,0:T(8,128)}, f32[1,7,64,128]{3,2,1,0:T(8,128)}) custom-call(f32[1,64,128]{2,1,0:T(8,128)} %density_in.1, f32[1,7,64,128]{3,2,1,0:T(8,128)} %fields_in.1, s32[64,128]{1,0:T(8,128)} %bitcast.11, s32[64,128]{1,0:T(8,128)} %bitcast.12, s32[1,128]{1,0:T(1,128)} %bitcast.13, s32[128,128]{1,0:T(8,128)} %bitcast.9, ...), custom_call_target="tpu_custom_call" | custom-call | tf_op jit(solution)/shard_map/cycle/pallas_call | solution.py:464
  60.6 1.4 %copy.12 = f32[1,64,128]{2,1,0:T(8,128)} copy(f32[1,64,128]{2,1,0:T(8,128)} %get-tuple-element.4) | data formatting | bytes 65536
  61.9 1.6 %copy.13 = f32[1,7,64,128]{3,2,1,0:T(8,128)} copy(f32[1,7,64,128]{3,2,1,0:T(8,128)} %get-tuple-element.5) | data formatting | bytes 458752

commit v3 on v2

--- a/solution.py
+++ b/solution.py
@@ -245,10 +245,7 @@
     @pl.when(mp < 3)
     def _():
         depart(halves[0], 0)
-        depart(halves[0] + 2, 0)
         pack(halves[1])
-        depart(lax.rem(x + 2, 4), 1)
-        depart(x, 1)
 
     @pl.when(magnetic)
     def _():
@@ -277,6 +274,10 @@
             return (iota((8, 128), 0) + b * 8) < counts
 
         slot_code[...] = invert(dst, used, lambda p: high, lambda p: ((lane >> 6) * 64 + p).astype(F32), 64).astype(I32)
+
+    @pl.when(mp < 3)
+    def _():
+        depart(halves[0] + 2, 0)
 
     for i in range(2):
         wait_for(halo_in.at[i], halo_recv.at[i])
@@ -308,6 +309,10 @@
     loop(1, PLANE // 2, give)
     spread[place] = total
 
+    @pl.when(mp < 3)
+    def _():
+        depart(lax.rem(x + 2, 4), 1)
+
     @pl.when(magnetic)
     def _():
         def used(b):
@@ -349,6 +354,10 @@
             push(mid.at[to_x, :, to], inbox.at[x, :, yc], fwd_send.at[t], inbox_recv.at[t], in_plane(to_x * YC + to))
 
         loop(first, YC, one)
+
+    @pl.when(mp < 3)
+    def _():
+        depart(x, 1)
 
     @pl.when(mp > 0)
     def _():

time: 63.8 us -> 52.1 us (0.82)
  the two profiles are of different devices: /device:TPU:257 before, /device:TPU:481 now
where the time goes in v3:
time: 52.1 us; the launch traced here: 51.9 us
  Pallas kernels  48.2 us (93%)
  local copies, waits for them, and re-layouts  3.02 us (6%)
  between operations  0.64 us (1%)
    pallas_call x1, Pallas kernels, local(): pl.pallas_call(cycle_kernel, out_shape=[jax.ShapeDtypeStruct((1, 64, 128)...  48.2 us
    unnamed x2, local copies, waits for them, and re-layouts  3.02 us

profile of v3, /device:TPU:481, one launch (start us, length us, event | category | flops | bytes accessed | tf_op | source)
XLA Modules:
  0.0 51.9 jit_solution(4768223407577043995)
XLA Ops:
  0.6 48.2 %cycle.1 = (f32[1,64,128]{2,1,0:T(8,128)}, f32[1,7,64,128]{3,2,1,0:T(8,128)}) custom-call(f32[1,64,128]{2,1,0:T(8,128)} %density_in.1, f32[1,7,64,128]{3,2,1,0:T(8,128)} %fields_in.1, s32[64,128]{1,0:T(8,128)} %bitcast.11, s32[64,128]{1,0:T(8,128)} %bitcast.12, s32[1,128]{1,0:T(1,128)} %bitcast.13, s32[128,128]{1,0:T(8,128)} %bitcast.9, ...), custom_call_target="tpu_custom_call" | custom-call | tf_op jit(solution)/shard_map/cycle/pallas_call | solution.py:473
  48.8 1.4 %copy.12 = f32[1,64,128]{2,1,0:T(8,128)} copy(f32[1,64,128]{2,1,0:T(8,128)} %get-tuple-element.4) | data formatting | bytes 65536
  50.2 1.6 %copy.13 = f32[1,7,64,128]{3,2,1,0:T(8,128)} copy(f32[1,7,64,128]{3,2,1,0:T(8,128)} %get-tuple-element.5) | data formatting | bytes 458752

commit v4 on v3

--- a/solution.py
+++ b/solution.py
@@ -107,7 +107,7 @@
 
 def cycle_kernel(
     density_in, fields_in, src_in, dst_in, count_in, owner_in, cell_in, response_in,
-    density_out, fields_out,
+    state_out,
     work, src, dst, recv_count, owner, cell, response, index, current, halo_out, halo_in,
     outbox, mid, inbox, table, contribution, rs, part, ar, full, spread, tile, line, lines, pot_part, pot,
     slot_code, iono_code,
@@ -413,30 +413,32 @@
         inbox[x, :, yc] = mid[x, :, yc]
         wait_for(inbox.at[pl.ds(0, 2)], inbox_recv.at[0])
         unpack(halves[0])
-        wait_for(inbox.at[pl.ds(0, 3), :, pl.ds(0, 5)], inbox_recv.at[1])
-        unpack(halves[1])
 
     @pl.when(magnetic)
     def _():
         wait_for(pot.at[pl.ds(0, PLANE - 1)], recv.at[4])
 
         def block(b):
-            at = pl.ds(pl.multiple_of(8 + b * 16, 8), 16)
             row = iono_code[pl.ds(b * 16, 16), :] - 1
             spot = iono_code[pl.ds(64 + b * 16, 16), :]
             (got,) = pick(
                 lambda r: (pot[r // 4, r % 4 : r % 4 + 1, :],), 128, row, spot, [jnp.zeros((16, 128), F32)]
             )
-            work[1, at, :] = work[1, at, :] + jnp.where(row >= 0, 0.5 * work[0, at, :] * got, 0.0)
+            current[pl.ds(b * 16, 16), :] = 0.5 * got
 
         loop(0, 4, block)
 
-    results = [
-        pltpu.make_async_copy(work.at[0, body], density_out.at[0], load.at[0]),
-        pltpu.make_async_copy(work.at[pl.ds(1, 7), body], fields_out.at[0], load.at[1]),
-    ]
-    for copy in results:
-        copy.start()
+    @pl.when(mp > 0)
+    def _():
+        wait_for(inbox.at[pl.ds(0, 3), :, pl.ds(0, 5)], inbox_recv.at[1])
+        unpack(halves[1])
+
+    @pl.when(magnetic)
+    def _():
+        work[1, body, :] = work[1, body, :] + work[0, body, :] * current[...]
+
+
+    state_out[...] = work[:, 8:72, :]
 
     for i in range(2):
         wait_for(halo_out.at[i], halo_send.at[i])
@@ -462,7 +464,15 @@
     def _():
         wait_for(lines.at[pl.ds(0, 8)], send.at[3])
 
-    for copy in results:
+
+def hand_out(state, density_out, fields_out, sem):
+    copies = [
+        pltpu.make_async_copy(state.at[0], density_out.at[0], sem.at[0]),
+        pltpu.make_async_copy(state.at[pl.ds(1, 7)], fields_out.at[0], sem.at[1]),
+    ]
+    for copy in copies:
+        copy.start()
+    for copy in copies:
         copy.wait()
 
 
@@ -470,11 +480,11 @@
     vmem = pltpu.VMEM
     dma = pltpu.SemaphoreType.DMA
     hbm = pl.BlockSpec(memory_space=pl.ANY)
-    return pl.pallas_call(
+    state = pl.pallas_call(
         cycle_kernel,
-        out_shape=[jax.ShapeDtypeStruct((1, 64, 128), F32), jax.ShapeDtypeStruct((1, 7, 64, 128), F32)],
+        out_shape=vmem((8, 64, 128), F32),
         in_specs=[hbm] * 8,
-        out_specs=[hbm] * 2,
+        out_specs=pl.BlockSpec(memory_space=vmem),
         scratch_shapes=[
             vmem((8, 80, 128), F32),
             vmem((64, 128), I32),
@@ -522,6 +532,7 @@
         density, fields, src_points[0, 0].T, dst_points[0, 0].T, recv_count[0],
         iono_owner.reshape(128, 128), iono_cell.reshape(128, 128), response,
     )
+    return state[:1], state[1:][None]
 
 
 def solution(mesh):

time: 52.1 us -> 48.4 us (0.929)
  Pallas kernels: 48.2 us -> 46.1 us
  local copies, waits for them, and re-layouts: 3.02 us -> 1.32 us
    unnamed x2 -> x0, local copies, waits for them, and re-layouts: 3.02 us -> none
    pallas_call x1, Pallas kernels: 48.2 us -> 46.1 us  [local(): pl.pallas_call(cycle_kernel, out_shape=vmem((8, 64, 128), F32), in_specs=...]
    broadcast_in_dim x0 -> x1, local copies, waits for them, and re-layouts: none -> 0.7 us  [local(): return (state[:1], state[1:][None])]
    slice x0 -> x1, local copies, waits for them, and re-layouts: none -> 0.62 us  [local(): return (state[:1], state[1:][None])]
where the time goes in v4:
time: 48.4 us; the launch traced here: 48.1 us
  Pallas kernels  46.1 us (95%)
  local copies, waits for them, and re-layouts  1.32 us (3%)
  between operations  0.64 us (1%)
    pallas_call x1, Pallas kernels, local(): pl.pallas_call(cycle_kernel, out_shape=vmem((8, 64, 128), F32), in_specs=...  46.1 us

profile of v4, /device:TPU:481, one launch (start us, length us, event | category | flops | bytes accessed | tf_op | source)
XLA Modules:
  0.0 48.1 jit_solution(10273222358953515727)
XLA Ops:
  0.6 46.1 %cycle.1 = f32[8,64,128]{2,1,0:T(8,128)S(1)} custom-call(f32[1,64,128]{2,1,0:T(8,128)} %density_in.1, f32[1,7,64,128]{3,2,1,0:T(8,128)} %fields_in.1, s32[64,128]{1,0:T(8,128)} %bitcast.13, s32[64,128]{1,0:T(8,128)} %bitcast.14, s32[1,128]{1,0:T(1,128)} %bitcast.15, s32[128,128]{1,0:T(8,128)} %bitcast.11, s32[128,128]{1,0:T(8,128)} %bitcast.12, ...), custom_call_target="tpu_custom_call" | custom-call | tf_op jit(solution)/shard_map/cycle/pallas_call | solution.py:483
  46.8 0.6 %slice.6 = f32[1,64,128]{2,1,0:T(8,128)} slice(f32[8,64,128]{2,1,0:T(8,128)S(1)} %cycle.1), slice={[0:1], [0:64], [0:128]} | slice | bytes 65536 | tf_op jit(solution)/shard_map/slice | solution.py:535
  47.4 0.7 %slice_bitcast_fusion = f32[1,7,64,128]{3,2,1,0:T(8,128)} fusion(f32[8,64,128]{2,1,0:T(8,128)S(1)} %cycle.1), kind=kLoop, calls=%fused_computation | loop fusion | bytes 458752 | tf_op jit(solution)/shard_map/broadcast_in_dim | solution.py:535

commit v5 on v4

--- a/solution.py
+++ b/solution.py
@@ -11,6 +11,7 @@
 SPACE = 128
 PLANE = 32
 LEVELS = 16
+ROUND = 2
 LAMBDA_STEP = 0.1
 F32 = jnp.float32
 I32 = jnp.int32
@@ -109,9 +110,9 @@
     density_in, fields_in, src_in, dst_in, count_in, owner_in, cell_in, response_in,
     state_out,
     work, src, dst, recv_count, owner, cell, response, index, current, halo_out, halo_in,
-    outbox, mid, inbox, table, contribution, rs, part, ar, full, spread, tile, line, lines, pot_part, pot,
+    outbox, mid, inbox, relay, table, contribution, rs, part, ar, full, spread, tile, line, lines, pot_part, pot,
     slot_code, iono_code,
-    load, halo_send, halo_recv, send, recv, out_send, mid_recv, fwd_send, inbox_recv,
+    load, halo_send, halo_recv, send, recv, out_send, mid_recv, fwd_send, inbox_recv, relay_send, relay_recv, known,
 ):
     mp = lax.axis_index("mp")
     space = lax.axis_index("space")
@@ -155,7 +156,8 @@
 
     after = (mp, lax.rem(space + 1, SPACE))
     before = (mp, lax.rem(space + SPACE - 1, SPACE))
-    loop(1, LEVELS, lambda i: greet(in_column(lax.rem(level + i, LEVELS))))
+    loop(1, 5, lambda i: greet(in_column(lax.rem(level + i, LEVELS))))
+    loop(1, 5, lambda i: greet(in_column(lax.rem(level + LEVELS - i, LEVELS))))
     loop(1, PLANE, lambda i: greet(in_plane(lax.rem(place + i, PLANE))))
     greet(after)
     greet(before)
@@ -214,20 +216,54 @@
 
         loop(0, 2, block)
 
-    def depart(to_x, t):
+    halves = (lax.rem(x + 1, 2), lax.rem(x, 2))
+    order = (halves[0], halves[0] + 2, lax.rem(x + 2, 4), x)
+
+    def round_count(from_z):
+        return jnp.where(from_z == 0, 2, jnp.where(from_z < 1 + ROUND, 1, 0))
+
+    def depart(quarter):
+        to_x = order[quarter]
+
         def one(i):
-            to = lax.rem(z + i, ZS)
-            push(outbox.at[to_x, to], mid.at[to_x, z], out_send, mid_recv.at[t], in_column((mp + 1) * ZS + to))
-
-        loop(0, ZS, one)
-
-    halves = (lax.rem(x + 1, 2), lax.rem(x, 2))
-
-    @pl.when(mp < 3)
-    def _():
-        pack(halves[0])
-
-    pl.semaphore_wait(barrier, LEVELS - 1 + PLANE - 1 + 2)
+            push(
+                outbox.at[to_x, i], mid.at[to_x, z], out_send, mid_recv.at[quarter // 2], in_column((mp + 1) * ZS + i)
+            )
+
+        loop(0, ZS - round_count(z), one)
+
+    def depart_round(t):
+        def one(i):
+            below = in_column(lax.rem(level + LEVELS - 7, LEVELS))
+            for quarter in (2 * t, 2 * t + 1):
+                push(outbox.at[order[quarter], 3 - i], relay.at[i, quarter], out_send, relay_recv.at[t], below)
+
+        loop(0, round_count(z), one)
+
+    relays = [
+        (jnp.logical_and(mp != 1, z == 1), pl.ds(0, 2)),
+        (jnp.logical_and(mp != 1, jnp.logical_and(z >= 2, z < 2 + ROUND)), pl.ds(0, 1)),
+    ]
+
+    def pass_on(t):
+        for here, slots in relays:
+
+            @pl.when(here)
+            def _(slots=slots):
+                wait_for(relay.at[slots, pl.ds(2 * t, 2)], relay_recv.at[t])
+
+                def one(i):
+                    to = in_column(lax.rem(mp + 3, 4) * ZS + 3 - i)
+                    for quarter in (2 * t, 2 * t + 1):
+                        push(relay.at[i, quarter], mid.at[order[quarter], z - 1], relay_send, mid_recv.at[t], to)
+
+                loop(0, slots.size, one)
+
+    pl.semaphore_wait(barrier, 8 + PLANE - 1 + 2)
+    for far in (4, LEVELS - 4):
+        pl.semaphore_signal(
+            known, inc=1, device_id=in_column(lax.rem(level + far, LEVELS)), device_id_type=MESH
+        )
 
     @pl.when(magnetic)
     def _():
@@ -244,7 +280,14 @@
 
     @pl.when(mp < 3)
     def _():
-        depart(halves[0], 0)
+        pack(halves[0])
+
+    pl.semaphore_wait(known, 2)
+
+    @pl.when(mp < 3)
+    def _():
+        depart_round(0)
+        depart(0)
         pack(halves[1])
 
     @pl.when(magnetic)
@@ -277,7 +320,9 @@
 
     @pl.when(mp < 3)
     def _():
-        depart(halves[0] + 2, 0)
+        depart_round(1)
+        depart(1)
+        depart(2)
 
     for i in range(2):
         wait_for(halo_in.at[i], halo_recv.at[i])
@@ -311,7 +356,9 @@
 
     @pl.when(mp < 3)
     def _():
-        depart(lax.rem(x + 2, 4), 1)
+        depart(3)
+
+    pass_on(0)
 
     @pl.when(magnetic)
     def _():
@@ -355,15 +402,13 @@
 
         loop(first, YC, one)
 
-    @pl.when(mp < 3)
-    def _():
-        depart(x, 1)
+    pass_on(1)
 
     @pl.when(mp > 0)
     def _():
         wait_for(mid.at[pl.ds(0, 2)], mid_recv.at[0])
-        forward(halves[0], 0, 0)
-        forward(halves[0] + 2, 0, 0)
+        forward(order[0], 0, 0)
+        forward(order[1], 0, 0)
 
     @pl.when(magnetic)
     def _():
@@ -408,35 +453,28 @@
     @pl.when(mp > 0)
     def _():
         wait_for(mid.at[pl.ds(0, 2)], mid_recv.at[1])
-        forward(lax.rem(x + 2, 4), 1, 0)
-        forward(x, 1, 1)
+        forward(order[2], 1, 0)
+        forward(order[3], 1, 1)
         inbox[x, :, yc] = mid[x, :, yc]
         wait_for(inbox.at[pl.ds(0, 2)], inbox_recv.at[0])
         unpack(halves[0])
+        wait_for(inbox.at[pl.ds(0, 3), :, pl.ds(0, 5)], inbox_recv.at[1])
+        unpack(halves[1])
 
     @pl.when(magnetic)
     def _():
         wait_for(pot.at[pl.ds(0, PLANE - 1)], recv.at[4])
 
         def block(b):
+            at = pl.ds(pl.multiple_of(8 + b * 16, 8), 16)
             row = iono_code[pl.ds(b * 16, 16), :] - 1
             spot = iono_code[pl.ds(64 + b * 16, 16), :]
             (got,) = pick(
                 lambda r: (pot[r // 4, r % 4 : r % 4 + 1, :],), 128, row, spot, [jnp.zeros((16, 128), F32)]
             )
-            current[pl.ds(b * 16, 16), :] = 0.5 * got
+            work[1, at, :] = work[1, at, :] + 0.5 * work[0, at, :] * got
 
         loop(0, 4, block)
-
-    @pl.when(mp > 0)
-    def _():
-        wait_for(inbox.at[pl.ds(0, 3), :, pl.ds(0, 5)], inbox_recv.at[1])
-        unpack(halves[1])
-
-    @pl.when(magnetic)
-    def _():
-        work[1, body, :] = work[1, body, :] + work[0, body, :] * current[...]
-
 
     state_out[...] = work[:, 8:72, :]
 
@@ -447,6 +485,12 @@
     @pl.when(mp < 3)
     def _():
         wait_for(mid, out_send)
+
+    for here, slots in relays:
+
+        @pl.when(here)
+        def _(slots=slots):
+            wait_for(relay.at[slots], relay_send)
 
     @pl.when(mp > 0)
     def _():
@@ -500,6 +544,7 @@
             vmem((4, ZS, YC, 4, 128), F32),
             vmem((4, ZS, YC, 4, 128), F32),
             vmem((4, ZS, YC, 4, 128), F32),
+            vmem((2, 4, YC, 4, 128), F32),
             vmem((8, 32, 128), F32),
             vmem((PLANE, 4, 128), F32),
             vmem((PLANE, 4, 128), F32),
@@ -523,6 +568,9 @@
             dma((2,)),
             dma((2,)),
             dma((2,)),
+            dma,
+            dma((2,)),
+            pltpu.SemaphoreType.REGULAR,
         ],
         compiler_params=pltpu.CompilerParams(
             collective_id=0, has_side_effects=True, vmem_limit_bytes=56 * 1024 * 1024

time: 48.4 us -> 45.6 us (0.942)
  Pallas kernels: 46.1 us -> 43 us
    pallas_call x1, Pallas kernels: 46.1 us -> 43 us  [local(): pl.pallas_call(cycle_kernel, out_shape=vmem((8, 64, 128), F32), in_specs=...]
where the time goes in v5:
time: 45.6 us; the launch traced here: 45 us
  Pallas kernels  43 us (94%)
  local copies, waits for them, and re-layouts  1.32 us (3%)
  between operations  0.64 us (1%)
    pallas_call x1, Pallas kernels, local(): pl.pallas_call(cycle_kernel, out_shape=vmem((8, 64, 128), F32), in_specs=...  43 us

profile of v5, /device:TPU:481, one launch (start us, length us, event | category | flops | bytes accessed | tf_op | source)
XLA Modules:
  0.0 45.0 jit_solution(14214789017171234698)
XLA Ops:
  0.6 43.0 %cycle.1 = f32[8,64,128]{2,1,0:T(8,128)S(1)} custom-call(f32[1,64,128]{2,1,0:T(8,128)} %density_in.1, f32[1,7,64,128]{3,2,1,0:T(8,128)} %fields_in.1, s32[64,128]{1,0:T(8,128)} %bitcast.13, s32[64,128]{1,0:T(8,128)} %bitcast.14, s32[1,128]{1,0:T(1,128)} %bitcast.15, s32[128,128]{1,0:T(8,128)} %bitcast.11, s32[128,128]{1,0:T(8,128)} %bitcast.12, ...), custom_call_target="tpu_custom_call" | custom-call | tf_op jit(solution)/shard_map/cycle/pallas_call | solution.py:527
  43.7 0.6 %slice.6 = f32[1,64,128]{2,1,0:T(8,128)} slice(f32[8,64,128]{2,1,0:T(8,128)S(1)} %cycle.1), slice={[0:1], [0:64], [0:128]} | slice | bytes 65536 | tf_op jit(solution)/shard_map/slice | solution.py:583
  44.3 0.7 %slice_bitcast_fusion = f32[1,7,64,128]{3,2,1,0:T(8,128)} fusion(f32[8,64,128]{2,1,0:T(8,128)S(1)} %cycle.1), kind=kLoop, calls=%fused_computation | loop fusion | bytes 458752 | tf_op jit(solution)/shard_map/broadcast_in_dim | solution.py:583

commit v6 on v5

--- a/solution.py
+++ b/solution.py
@@ -127,6 +127,18 @@
     def in_plane(p):
         return (mp, (lax.div(p, YC) * ZS + z) * YC + lax.rem(p, YC))
 
+    def elsewhere_in_plane(body):
+        steps = sorted(
+            ((dx, dy) for dx in range(4) for dy in range(4)),
+            key=lambda d: -(min(d[0], 4 - d[0]) + min(d[1], 4 - d[1])),
+        )
+        core = lax.rem(yc, 2)
+        for dx, dy in steps:
+            chip = lax.rem(x + dx, 4) * YC + lax.rem(lax.div(yc, 2) + dy, 4) * 2
+            if dx or dy:
+                body(chip + core)
+            body(chip + 1 - core)
+
     def in_column(l):
         return (lax.div(l, ZS), (x * ZS + lax.rem(l, ZS)) * YC + yc)
 
@@ -156,11 +168,15 @@
 
     after = (mp, lax.rem(space + 1, SPACE))
     before = (mp, lax.rem(space + SPACE - 1, SPACE))
-    loop(1, 5, lambda i: greet(in_column(lax.rem(level + i, LEVELS))))
-    loop(1, 5, lambda i: greet(in_column(lax.rem(level + LEVELS - i, LEVELS))))
-    loop(1, PLANE, lambda i: greet(in_plane(lax.rem(place + i, PLANE))))
     greet(after)
     greet(before)
+    for i in (4, 3):
+        greet(in_column(lax.rem(level + i, LEVELS)))
+        greet(in_column(lax.rem(level + LEVELS - i, LEVELS)))
+    elsewhere_in_plane(lambda p: greet(in_plane(p)))
+    for i in (2, 1):
+        greet(in_column(lax.rem(level + i, LEVELS)))
+        greet(in_column(lax.rem(level + LEVELS - i, LEVELS)))
 
     low = iota((8, 128), 1) < 64
     lane = iota((1, 128), 1)
@@ -267,12 +283,9 @@
 
     @pl.when(magnetic)
     def _():
-        def one(i):
-            to = lax.rem(place + i, PLANE)
-            push(contribution.at[to], rs.at[place], send.at[0], recv.at[0], in_plane(to))
-
-        loop(PLANE // 2, PLANE, one)
-        loop(1, PLANE // 2, one)
+        elsewhere_in_plane(
+            lambda p: push(contribution.at[p], rs.at[place], send.at[0], recv.at[0], in_plane(p))
+        )
         rs[place] = contribution[place]
 
     push(halo_out.at[0], halo_in.at[1], halo_send.at[0], halo_recv.at[1], before)
@@ -298,11 +311,8 @@
             total = total + rs[i]
         part[...] = total
 
-        def one(i):
+        for i in (8, 7, 9, 6, 10, 5, 11, 4, 12, 3, 13, 2, 14, 1, 15):
             push(part, ar.at[level - 8], send.at[1], recv.at[1], in_column(lax.rem(level + i, LEVELS)))
-
-        loop(8, LEVELS, one)
-        loop(1, 8, one)
         ar[level - 8] = total
 
     loads[5].wait()
@@ -347,11 +357,7 @@
         total = total + ar[i]
     full[...] = total
 
-    def give(i):
-        push(full, spread.at[place], send.at[2], recv.at[2], in_plane(lax.rem(place + i, PLANE)))
-
-    loop(PLANE // 2, PLANE, give)
-    loop(1, PLANE // 2, give)
+    elsewhere_in_plane(lambda p: push(full, spread.at[place], send.at[2], recv.at[2], in_plane(p)))
     spread[place] = total
 
     @pl.when(mp < 3)
@@ -396,11 +402,15 @@
         loop(0, 8, report)
 
     def forward(to_x, t, first):
-        def one(i):
-            to = lax.rem(yc + i, YC)
-            push(mid.at[to_x, :, to], inbox.at[x, :, yc], fwd_send.at[t], inbox_recv.at[t], in_plane(to_x * YC + to))
-
-        loop(first, YC, one)
+        core = lax.rem(yc, 2)
+        for dy in (2, 1, 3, 0):
+            for dc in (0, 1):
+                if first and dy + dc == 0:
+                    continue
+                to = lax.rem(lax.div(yc, 2) + dy, 4) * 2 + lax.rem(core + dc, 2)
+                push(
+                    mid.at[to_x, :, to], inbox.at[x, :, yc], fwd_send.at[t], inbox_recv.at[t], in_plane(to_x * YC + to)
+                )
 
     pass_on(1)
 
@@ -422,11 +432,7 @@
         mine = jnp.concatenate(rows, axis=0)
         pot_part[...] = mine
 
-        def one(i):
-            push(pot_part, pot.at[place], send.at[4], recv.at[4], in_plane(lax.rem(place + i, PLANE)))
-
-        loop(PLANE // 2, PLANE, one)
-        loop(1, PLANE // 2, one)
+        elsewhere_in_plane(lambda p: push(pot_part, pot.at[place], send.at[4], recv.at[4], in_plane(p)))
         pot[place] = mine
 
     def unpack(half):

time: 45.6 us -> 44.7 us (0.980)
  Pallas kernels: 43 us -> 42.1 us
    pallas_call x1, Pallas kernels: 43 us -> 42.1 us  [local(): pl.pallas_call(cycle_kernel, out_shape=vmem((8, 64, 128), F32), in_specs=...]
where the time goes in v6:
time: 44.7 us; the launch traced here: 44.1 us
  Pallas kernels  42.1 us (94%)
  local copies, waits for them, and re-layouts  1.32 us (3%)
  between operations  0.64 us (1%)
    pallas_call x1, Pallas kernels, local(): pl.pallas_call(cycle_kernel, out_shape=vmem((8, 64, 128), F32), in_specs=...  42.1 us

profile of v6, /device:TPU:481, one launch (start us, length us, event | category | flops | bytes accessed | tf_op | source)
XLA Modules:
  0.0 44.1 jit_solution(8840466287666694945)
XLA Ops:
  0.6 42.1 %cycle.1 = f32[8,64,128]{2,1,0:T(8,128)S(1)} custom-call(f32[1,64,128]{2,1,0:T(8,128)} %density_in.1, f32[1,7,64,128]{3,2,1,0:T(8,128)} %fields_in.1, s32[64,128]{1,0:T(8,128)} %bitcast.13, s32[64,128]{1,0:T(8,128)} %bitcast.14, s32[1,128]{1,0:T(1,128)} %bitcast.15, s32[128,128]{1,0:T(8,128)} %bitcast.11, s32[128,128]{1,0:T(8,128)} %bitcast.12, ...), custom_call_target="tpu_custom_call" | custom-call | tf_op jit(solution)/shard_map/cycle/pallas_call | solution.py:533
  42.7 0.6 %slice.6 = f32[1,64,128]{2,1,0:T(8,128)} slice(f32[8,64,128]{2,1,0:T(8,128)S(1)} %cycle.1), slice={[0:1], [0:64], [0:128]} | slice | bytes 65536 | tf_op jit(solution)/shard_map/slice | solution.py:589
  43.4 0.7 %slice_bitcast_fusion = f32[1,7,64,128]{3,2,1,0:T(8,128)} fusion(f32[8,64,128]{2,1,0:T(8,128)S(1)} %cycle.1), kind=kLoop, calls=%fused_computation | loop fusion | bytes 458752 | tf_op jit(solution)/shard_map/broadcast_in_dim | solution.py:589

commit v7 on v6

--- a/solution.py
+++ b/solution.py
@@ -293,15 +293,20 @@
 
     @pl.when(mp < 3)
     def _():
-        pack(halves[0])
-
-    pl.semaphore_wait(known, 2)
-
-    @pl.when(mp < 3)
-    def _():
-        depart_round(0)
-        depart(0)
-        pack(halves[1])
+        def each(t):
+            pack(lax.rem(x + 1 + t, 2))
+
+            @pl.when(t == 0)
+            def _():
+                pl.semaphore_wait(known, 2)
+                depart_round(0)
+                depart(0)
+
+        loop(0, 2, each)
+
+    @pl.when(mp == 3)
+    def _():
+        pl.semaphore_wait(known, 2)
 
     @pl.when(magnetic)
     def _():
@@ -462,10 +467,19 @@
         forward(order[2], 1, 0)
         forward(order[3], 1, 1)
         inbox[x, :, yc] = mid[x, :, yc]
-        wait_for(inbox.at[pl.ds(0, 2)], inbox_recv.at[0])
-        unpack(halves[0])
-        wait_for(inbox.at[pl.ds(0, 3), :, pl.ds(0, 5)], inbox_recv.at[1])
-        unpack(halves[1])
+
+        def each(t):
+            @pl.when(t == 0)
+            def _():
+                wait_for(inbox.at[pl.ds(0, 2)], inbox_recv.at[0])
+
+            @pl.when(t == 1)
+            def _():
+                wait_for(inbox.at[pl.ds(0, 3), :, pl.ds(0, 5)], inbox_recv.at[1])
+
+            unpack(lax.rem(x + 1 + t, 2))
+
+        loop(0, 2, each)
 
     @pl.when(magnetic)
     def _():

time: 44.7 us -> 44.7 us (level)
  no operation moved by 1% of the time
where the time goes in v7:
time: 44.7 us; the launch traced here: 44 us
  Pallas kernels  42.1 us (94%)
  local copies, waits for them, and re-layouts  1.32 us (3%)
  between operations  0.64 us (1%)
    pallas_call x1, Pallas kernels, local(): pl.pallas_call(cycle_kernel, out_shape=vmem((8, 64, 128), F32), in_specs=...  42.1 us

profile of v7, /device:TPU:481, one launch (start us, length us, event | category | flops | bytes accessed | tf_op | source)
XLA Modules:
  0.0 44.0 jit_solution(5683465679852149729)
XLA Ops:
  0.6 42.1 %cycle.1 = f32[8,64,128]{2,1,0:T(8,128)S(1)} custom-call(f32[1,64,128]{2,1,0:T(8,128)} %density_in.1, f32[1,7,64,128]{3,2,1,0:T(8,128)} %fields_in.1, s32[64,128]{1,0:T(8,128)} %bitcast.13, s32[64,128]{1,0:T(8,128)} %bitcast.14, s32[1,128]{1,0:T(1,128)} %bitcast.15, s32[128,128]{1,0:T(8,128)} %bitcast.11, s32[128,128]{1,0:T(8,128)} %bitcast.12, ...), custom_call_target="tpu_custom_call" | custom-call | tf_op jit(solution)/shard_map/cycle/pallas_call | solution.py:547
  42.7 0.6 %slice.6 = f32[1,64,128]{2,1,0:T(8,128)} slice(f32[8,64,128]{2,1,0:T(8,128)S(1)} %cycle.1), slice={[0:1], [0:64], [0:128]} | slice | bytes 65536 | tf_op jit(solution)/shard_map/slice | solution.py:603
  43.3 0.7 %slice_bitcast_fusion = f32[1,7,64,128]{3,2,1,0:T(8,128)} fusion(f32[8,64,128]{2,1,0:T(8,128)S(1)} %cycle.1), kind=kLoop, calls=%fused_computation | loop fusion | bytes 458752 | tf_op jit(solution)/shard_map/broadcast_in_dim | solution.py:603
